TPU v7x, 32 devices: a whole 2x2x4 slice. The times are simulated.
32 devices in a mesh: block: 4 (over x, core), seq: 2 (over y), mp: 4 (over z).
Axes of the slice: x: 2, y: 2, z: 4, core: 2. Of those that a mesh axis runs over, the one named last changes fastest.
Arguments:
- noisy_latent: float32 [4, 256, 64], P('block', 'seq'), may hold values from -6 to 6
- step_index: int32 [4, 256], P('block', 'seq'), may hold values from 0 to 29
- frame_offset: int32 [4], replicated, may hold values from 0 to 63
- query_input: bfloat16 [4, 256, 2560], P('block', 'seq', 'mp'), may hold values from -6 to 6
- key_input: bfloat16 [4, 256, 2560], P('block', 'seq', 'mp'), may hold values from -6 to 6
- value_input: bfloat16 [4, 256, 2560], P('block', 'seq', 'mp'), may hold values from -6 to 6
- context_keys: bfloat16 [4, 128, 2560], P('block', 'seq', 'mp'), may hold values from -6 to 6
- context_values: bfloat16 [4, 128, 2560], P('block', 'seq', 'mp'), may hold values from -6 to 6
- query_gain: float32 [2560], P('mp'), may hold values from 1 to 2
- key_gain: float32 [2560], P('mp'), may hold values from 1 to 2
- gate_table: float32 [30, 2560], P(None, 'mp'), may hold values from -4 to 4
- head_weight: bfloat16 [2560, 64], P('mp'), may hold values from -0.5 to 0.5
- conv_weight: bfloat16 [3, 3, 3, 16, 384], P(None, None, None, None, 'mp'), may hold values from -0.3125 to 0.3125
- conv_bias: float32 [384], P('mp'), may hold values from -3 to 3
Outputs:
- next_latent: float32 [4, 256, 64], P('block', 'seq')
- decoded: bfloat16 [4, 2, 4, 128, 384], P('block', None, None, 'seq', 'mp')
All inputs are finite; a program needn't handle non-finite values.
Results may differ from a plain program's by a relative error of at most 0.0078.
Values may be sent and summed in bfloat16 or wider, within the bound.
A program may use at most 64 MiB of HBM per device.

v0:
```python
import math

import jax
import jax.numpy as jnp
import numpy as np
from jax import lax
from jax.sharding import PartitionSpec as P

HEADS = 20
HD = 128
LAT = 16
STEPS = 30
FRAMES = 2
PW = 64
RDEV = 2


shift_factor = 8.0


def passed_along(x, axis, by):
    devices = lax.axis_size(axis)
    pairs = [(i, i + by) for i in range(devices) if 0 <= i + by < devices]
    return lax.ppermute(x, axis, pairs)


def padded_2(x, sides, width):
    for axis, dim in sides:
        devices, length = (lax.axis_size(axis), x.shape[dim])
        up = [(i, (i + 1) % devices) for i in range(devices - 1)]
        down = [(j, i) for i, j in up]
        last = lax.slice_in_dim(x, length - width, length, axis=dim)
        initial = lax.slice_in_dim(x, 0, width, axis=dim)
        before = lax.ppermute(last, axis, up)
        after = lax.ppermute(initial, axis, down)
        x = jnp.concatenate([before, x, after], axis=dim)
    return x


def frequency_rows():
    pairs_time = (HD - 4 * (HD // 6)) // 2
    pairs_side = HD // 6
    time_part = 10000.0 ** (-np.arange(pairs_time) / pairs_time)
    side_part = 10000.0 ** (-np.arange(pairs_side) / pairs_side)
    blank_time = np.zeros(pairs_time)
    blank_side = np.zeros(pairs_side)
    along_time = np.concatenate([time_part, blank_side, blank_side])
    along_rows = np.concatenate([blank_time, side_part, blank_side])
    along_cols = np.concatenate([blank_time, blank_side, side_part])
    return (
        jnp.asarray(along_time, jnp.float32),
        jnp.asarray(along_rows, jnp.float32),
        jnp.asarray(along_cols, jnp.float32),
    )


def square_total(raw_input):
    values = raw_input.astype(jnp.float32)
    return jnp.sum(values * values, axis=1)


def normalize_rotate(raw_input, total_sq, gain_row, time_pos, row_pos, col_pos):
    amount = raw_input.shape[0]
    head_count = raw_input.shape[1] // HD
    values = raw_input.astype(jnp.float32).reshape(amount, head_count, HD)
    factor = lax.rsqrt(total_sq / (HEADS * HD) + 1e-06)[:, None, None]
    values = values * factor * gain_row.reshape(1, head_count, HD)
    along_time, along_rows, along_cols = frequency_rows()
    angles = (
        time_pos[:, None] * along_time[None, :]
        + row_pos[:, None] * along_rows[None, :]
        + col_pos[:, None] * along_cols[None, :]
    )
    cosine = jnp.cos(angles)[:, None, :]
    sine_part = jnp.sin(angles)[:, None, :]
    paired = values.reshape(amount, head_count, HD // 2, 2)
    real_part = paired[..., 0]
    imag_part = paired[..., 1]
    turned = jnp.stack(
        [real_part * cosine - imag_part * sine_part, real_part * sine_part + imag_part * cosine],
        axis=-1,
    )
    return turned.reshape(amount, head_count * HD).astype(jnp.bfloat16)


def noise_level(level_now):
    remain = 1.0 - level_now / STEPS
    return shift_factor * remain / (1.0 + (shift_factor - 1.0) * remain)


def lift_tokens(tokens, columns, grid_rows):
    shaped = tokens.reshape(FRAMES, grid_rows, columns, 2, 2, LAT)
    return shaped.transpose(0, 1, 3, 2, 4, 5).reshape(FRAMES, 2 * grid_rows, 2 * columns, LAT)


def convolve(padded, conv_weight, conv_bias):
    frames_out = padded.shape[0] - 2
    height = padded.shape[1] - 2
    span_cols = padded.shape[2] - 2
    pieces = []
    for time_tap in range(3):
        for row_tap in range(3):
            for col_tap in range(3):
                pieces.append(
                    padded[
                        time_tap : time_tap + frames_out,
                        row_tap : row_tap + height,
                        col_tap : col_tap + span_cols,
                        :,
                    ]
                )
    stacked = jnp.stack(pieces, axis=3).reshape(frames_out * height * span_cols, 27 * LAT)
    flat_weight = conv_weight.reshape(27 * LAT, conv_weight.shape[-1])
    summed = jnp.dot(stacked, flat_weight, preferred_element_type=jnp.float32)
    summed = summed + conv_bias[None, :]
    return summed.astype(jnp.bfloat16).reshape(frames_out, height, span_cols, -1)


def with_cache(slab):
    earlier = passed_along(slab, "block", 1)
    return jnp.concatenate([earlier, slab], 0)


def body(
    noisy_latent,
    step_index,
    frame_offset,
    query_input,
    key_input,
    value_input,
    context_keys,
    context_values,
    query_gain,
    key_gain,
    gate_table,
    head_weight,
    conv_weight,
    conv_bias,
):
    clip_pos = lax.axis_index("block")
    seq_pos = lax.axis_index("seq")
    seq_count = lax.axis_size("seq")
    tok_rows = query_input.shape[1]
    ctx_rows = context_keys.shape[1]
    local_width = query_input.shape[2]
    local_heads = local_width // HD
    grid_rows = RDEV * seq_count // FRAMES
    inverse_root = 1.0 / math.sqrt(HD)
    relayed = passed_along(jnp.stack([context_keys[0], context_values[0]]), "block", 1)
    query_sq, key_sq, prior_sq = lax.psum(
        (square_total(query_input[0]), square_total(key_input[0]), square_total(relayed[0])), "mp"
    )
    token_ids = seq_pos * tok_rows + jnp.arange(tok_rows, dtype=jnp.int32)
    frame_ids = token_ids // (grid_rows * PW)
    row_ids = (token_ids // PW % grid_rows).astype(jnp.float32)
    col_ids = (token_ids % PW).astype(jnp.float32)
    own_offset = lax.dynamic_index_in_dim(frame_offset, clip_pos, 0, keepdims=False)
    prior_offset = lax.dynamic_index_in_dim(
        frame_offset, jnp.maximum(clip_pos - 1, 0), 0, keepdims=False
    )
    moment = (own_offset + frame_ids).astype(jnp.float32)
    queries = normalize_rotate(query_input[0], query_sq, query_gain, moment, row_ids, col_ids)
    own_keys = normalize_rotate(key_input[0], key_sq, key_gain, moment, row_ids, col_ids)
    own_values = value_input[0]
    context_ids = seq_pos * ctx_rows + jnp.arange(ctx_rows, dtype=jnp.int32)
    context_moment = jnp.zeros((ctx_rows,), jnp.float32) + (prior_offset + FRAMES - 1).astype(
        jnp.float32
    )
    prior_rot = normalize_rotate(
        relayed[0],
        prior_sq,
        key_gain,
        context_moment,
        (context_ids // PW).astype(jnp.float32),
        (context_ids % PW).astype(jnp.float32),
    )
    prior_values = relayed[1]
    keep_prior = (clip_pos > 0).astype(jnp.float32)
    start_state = (
        jnp.zeros((tok_rows, local_width), jnp.float32),
        jnp.zeros((tok_rows, local_heads), jnp.float32),
    )
    joint_rows = tok_rows + ctx_rows
    joint_keys = jnp.concatenate([own_keys, prior_rot], 0)
    joint_values = jnp.concatenate([own_values, prior_values], 0)
    piece = (
        lax.all_gather(joint_keys, "seq", axis=0, tiled=True),
        lax.all_gather(joint_values, "seq", axis=0, tiled=True),
    )
    local_rows = jnp.arange(piece[0].shape[0], dtype=jnp.int32) % joint_rows
    row_keep = jnp.where(local_rows < tok_rows, 1.0, keep_prior)
    key_piece = piece[0]
    value_piece = piece[1]

    def per_head(head_slot, state):
        numer, denom = state
        query_head = lax.dynamic_slice_in_dim(queries, head_slot * HD, HD, 1)
        key_head = lax.dynamic_slice_in_dim(key_piece, head_slot * HD, HD, 1)
        value_head = lax.dynamic_slice_in_dim(value_piece, head_slot * HD, HD, 1)
        scores = (
            jnp.einsum("qd,kd->qk", query_head, key_head, preferred_element_type=jnp.float32)
            * inverse_root
        )
        expon = jnp.exp(scores) * row_keep[None, :]
        added = jnp.dot(expon.astype(jnp.bfloat16), value_head, preferred_element_type=jnp.float32)
        old_numer = lax.dynamic_slice_in_dim(numer, head_slot * HD, HD, 1)
        numer = lax.dynamic_update_slice_in_dim(numer, old_numer + added, head_slot * HD, 1)
        old_denom = lax.dynamic_slice_in_dim(denom, head_slot, 1, 1)
        denom = lax.dynamic_update_slice_in_dim(
            denom, old_denom + jnp.sum(expon, axis=1, keepdims=True), head_slot, 1
        )
        return (numer, denom)

    state = lax.fori_loop(0, local_heads, per_head, start_state)
    numer, denom = state
    attention = (numer.reshape(tok_rows, local_heads, HD) / denom[:, :, None]).reshape(
        tok_rows, local_width
    )
    one_hot = (step_index[0][:, None] == jnp.arange(STEPS, dtype=jnp.int32)[None, :]).astype(
        jnp.float32
    )
    gate_rows = jnp.dot(one_hot, gate_table, precision=lax.Precision.HIGHEST)
    gated_out = (attention * gate_rows).astype(jnp.bfloat16)
    partial_sum = jnp.dot(gated_out, head_weight, preferred_element_type=jnp.float32)
    velocity = lax.psum(partial_sum, "mp")
    level_now = step_index[0].astype(jnp.float32)
    now_sigma = noise_level(level_now)[:, None]
    next_sigma = noise_level(level_now + 1.0)[:, None]
    latent_now = noisy_latent[0]
    next_latent = latent_now + (next_sigma - now_sigma) * velocity
    clean_tokens = (latent_now - now_sigma * velocity).astype(jnp.bfloat16)
    slab_cols = PW // seq_count
    rows_local = clean_tokens.reshape(RDEV, PW, clean_tokens.shape[1])
    moved = lax.all_to_all(rows_local, "seq", split_axis=1, concat_axis=0, tiled=True)
    slab = lift_tokens(moved, slab_cols, grid_rows)
    framed = padded_2(with_cache(slab), (("seq", 2),), 1)
    framed = jnp.pad(framed, ((0, 0), (1, 1), (0, 0), (0, 0)))
    decoded = convolve(framed, conv_weight, conv_bias)
    return (next_latent[None], decoded[None])


def solution(mesh):
    return jax.shard_map(
        body,
        mesh=mesh,
        in_specs=(
            P("block", "seq", None),
            P("block", "seq"),
            P(),
            P("block", "seq", "mp"),
            P("block", "seq", "mp"),
            P("block", "seq", "mp"),
            P("block", "seq", "mp"),
            P("block", "seq", "mp"),
            P("mp"),
            P("mp"),
            P(None, "mp"),
            P("mp", None),
            P(None, None, None, None, "mp"),
            P("mp"),
        ),
        out_specs=(P("block", "seq", None), P("block", None, None, "seq", "mp")),
        check_vma=False,
    )
```

profile of v0, /device:TPU:0, one launch (start us, length us, event | category | flops | bytes accessed | tf_op | source)
XLA Modules:
  0.0 109.4 jit_solution(6795623228385123150)
XLA Ops:
  0.6 1.1 copy.153
  1.7 1.1 copy.154
  2.9 2.4 %collective-permute-start = (bf16[2,64,640]{1,2,0:T(8,128)(2,1)S(1)}, bf16[2,64,640]{1,2,0:T(8,128)(2,1)S(1)}, u32[]{:S(2)}, u32[]{:S(2)}) collective-permute-start(bf16[2,64,640]{1,2,0:T(8,128)(2,1)S(1)} %pad_maximum_fusion), channel_id=1, source_target_pairs={{0,8},{8,16},{16,24},{1,9},{9,17},{17,25},{2,10},{10,18},{18,26},{... | collective-permute-start | bytes 491528 | tf_op jit(solution)/shard_map/ppermute | solution.py:24
  5.3 1.3 %fusion.64 = (s32[1]{0:T(128)}, s32[1]{0:T(128)}) fusion(s32[4]{0:T(128)} %param.27, s32[]{:T(128)S(6)} %max.3, s32[]{:T(128)S(6)} %select_n.86), kind=kLoop, calls=%fused_computation.155 | loop fusion | bytes 24 | tf_op jit(solution)/shard_map/jit(dynamic_index_in_dim)/dynamic_slice | solution.py:158
  7.9 0.7 divide_subtract_fusion
  8.6 1.1 copy.151
  9.7 0.7 broadcast_multiply_fusion
  10.4 0.9 fusion.53
  11.2 0.9 fusion.55
  12.2 1.1 copy.152
  13.3 0.8 mul.464
  14.2 0.8 mul.442
  15.2 12.8 %all-reduce.1 = (f32[128]{0:T(128)S(1)}, f32[64]{0:T(128)S(1)}, f32[128]{0:T(128)S(1)}) all-reduce(f32[128]{0:T(128)S(1)} %multiply_reduce_fusion.2, f32[64]{0:T(128)S(1)} %multiply_reduce_fusion, f32[128]{0:T(128)S(1)} %multiply_reduce_fusion.1), channel_id=1, replica_groups=mesh['block'=4,'seq'=2,'mp'=4] {'mp'}, use_global_device_ids=true, to_apply=%region_1.0 | all-reduce | flops 320 | bytes 2560 | tf_op jit(solution)/shard_map/psum | solution.py:150
  29.1 0.9 subtract_convert_fusion.1
  31.9 8.3 %all_gather.7 = bf16[384,640]{1,0:T(8,128)(2,1)S(1)} all-gather(bf16[192,640]{1,0:T(8,128)(2,1)S(1)} %pad_maximum_fusion.3), channel_id=1, replica_groups=mesh['block'=4,'seq'=2,'mp'=4] {'seq'}, dimensions={0}, use_global_device_ids=true | all-gather | bytes 737280 | tf_op jit(solution)/shard_map/all_gather | solution.py:188
  40.2 7.5 %all_gather.6 = bf16[384,640]{1,0:T(8,128)(2,1)S(1)} all-gather(bf16[192,640]{1,0:T(8,128)(2,1)S(1)} %copy.155), channel_id=1, replica_groups=mesh['block'=4,'seq'=2,'mp'=4] {'seq'}, dimensions={0}, use_global_device_ids=true | all-gather | bytes 737280 | tf_op jit(solution)/shard_map/all_gather | solution.py:187
  48.1 2.9 %while.16 = (s32[]{:T(128)}, f32[128,640]{1,0:T(8,128)S(1)}, f32[128,5]{0,1:T(8,128)S(1)}, bf16[128,640]{0,1:T(8,128)(2,1)S(1)}, bf16[384,640]{1,0:T(8,128)(2,1)...) while((s32[]{:T(128)}, f32[128,640]{1,0:T(8,128)S(1)}, ...), condition=%wide.region_8.9_spmd.clone, body=%wide.region_6.8_spmd.clone.sunk | while | flops 25381892 | bytes 565935 | solution.py:214
  51.8 16.1 %psum.31 = f32[128,64]{0,1:T(8,128)S(1)} all-reduce(f32[128,64]{0,1:T(8,128)S(1)} %fusion.65), channel_id=1, replica_groups=mesh['block'=4,'seq'=2,'mp'=4] {'mp'}, use_global_device_ids=true, to_apply=%region_9.10 | all-reduce | flops 8192 | bytes 65536 | tf_op jit(solution)/shard_map/psum | solution.py:225
  68.8 6.4 %all_to_all.15 = bf16[2,2,2048]{2,1,0:T(2,128)(2,1)S(1)} all-to-all(bf16[2,2,2048]{2,1,0:T(2,128)(2,1)S(1)} %reshape.581), channel_id=1, replica_groups=mesh['block'=4,'seq'=2,'mp'=4] {'seq'}, dimensions={0} | all-to-all | bytes 32768 | tf_op jit(solution)/shard_map/all_to_all | solution.py:234
  75.6 1.3 %collective-permute-start.1 = (bf16[2,4,64,16]{3,2,1,0:T(8,128)(2,1)S(1)}, bf16[2,4,64,16]{3,2,1,0:T(8,128)(2,1)S(1)}, u32[]{:S(2)}, u32[]{:S(2)}) collective-permute-start(bf16[2,4,64,16]{3,2,1,0:T(8,128)(2,1)S(1)} %bitcast.158), channel_id=1, source_target_pairs={{0,8},{8,16},{16,24},{1,9},{9,17},{17,25},{2,10},{10,18},{18,26},{... | collective-permute-start | bytes 49160 | tf_op jit(solution)/shard_map/ppermute | solution.py:24
  76.9 1.0 collective-permute-done.1
  77.8 1.9 %collective-permute-start.2 = (bf16[4,4,1,16]{3,2,1,0:T(2,128)(2,1)S(1)}, bf16[4,4,1,16]{3,2,1,0:T(2,128)(2,1)S(1)}, u32[]{:S(2)}, u32[]{:S(2)}) collective-permute-start(bf16[4,4,1,16]{3,2,1,0:T(2,128)(2,1)S(1)} %get-tuple-element.221), channel_id=1, source_target_pairs={{0,4},{1,5},{2,6},{3,7},{8,12},{9,13},{10,14},{11,15},{16,20},{17,... | collective-permute-start | bytes 1544 | tf_op jit(solution)/shard_map/ppermute | solution.py:34
  79.8 1.3 %collective-permute-start.3 = (bf16[4,4,1,16]{3,2,1,0:T(2,128)(2,1)S(1)}, bf16[4,4,1,16]{3,2,1,0:T(2,128)(2,1)S(1)}, u32[]{:S(2)}, u32[]{:S(2)}) collective-permute-start(bf16[4,4,1,16]{3,2,1,0:T(2,128)(2,1)S(1)} %get-tuple-element.222), channel_id=1, source_target_pairs={{4,0},{5,1},{6,2},{7,3},{12,8},{13,9},{14,10},{15,11},{20,16},{21,... | collective-permute-start | bytes 1544 | tf_op jit(solution)/shard_map/ppermute | solution.py:35
  81.1 4.2 %collective-permute-done.3 = bf16[4,4,1,16]{3,2,1,0:T(2,128)(2,1)S(1)} collective-permute-done((bf16[4,4,1,16]{3,2,1,0:T(2,128)(2,1)S(1)}, bf16[4,4,1,16]{3,2,1,0:T(2,128)(2,1)S(1)}, u32[]{:S(2)}, u32[]{:S(2)}) %collective-permute-start.3) | collective-permute-done | bytes 544 | tf_op jit(solution)/shard_map/ppermute | solution.py:35
  86.1 0.7 fusion.47
  86.8 0.7 fusion.46
  87.6 0.7 fusion.45
  88.9 0.7 fusion.44
  89.6 0.7 fusion.43
  90.3 0.7 fusion.42
  91.0 0.7 fusion.41
  91.6 0.7 fusion.40
  92.3 0.7 fusion.39
  93.0 0.7 fusion.38
  93.7 0.7 fusion.37
  94.3 0.7 fusion.36
  95.0 0.7 fusion.34
  95.7 0.7 fusion.33
  96.4 0.7 fusion.32
  97.1 0.7 fusion.31
  97.7 0.7 fusion.30
  98.4 0.7 fusion.29
  99.1 0.7 fusion.28
  101.1 0.7 fusion.26
  102.5 0.7 fusion.24
  103.2 0.7 fusion.23
  103.8 4.0 %copy.164 = bf16[2,4,64,27,16]{2,1,0,4,3:T(4,128)(2,1)S(1)} copy(bf16[2,4,64,27,16]{4,2,1,0,3:T(8,128)(2,1)} %fusion.23) | data formatting | bytes 884736 | tf_op jit(solution)/shard_map/stack | solution.py:112
  108.6 0.8 copy.165
  (86 shorter events, 13.5 us)
Async XLA Ops:
  0.6 107.7 %copy-start = (bf16[3,3,3,16,96]{4,3,2,1,0:T(8,128)(2,1)S(1)}, bf16[3,3,3,16,96]{4,3,2,1,0:T(8,128)(2,1)}, u32[]{:S(2)}) copy-start(bf16[3,3,3,16,96]{4,3,2,1,0:T(8,128)(2,1)} %param.37) | copy-start | bytes 248836
  2.9 12.3 %collective-permute-start = (bf16[2,64,640]{1,2,0:T(8,128)(2,1)S(1)}, bf16[2,64,640]{1,2,0:T(8,128)(2,1)S(1)}, u32[]{:S(2)}, u32[]{:S(2)}) collective-permute-start(bf16[2,64,640]{1,2,0:T(8,128)(2,1)S(1)} %pad_maximum_fusion), channel_id=1, source_target_pairs={{0,8},{8,16},{16,24},{1,9},{9,17},{17,25},{2,10},{10,18},{18,26},{... | collective-permute-start | bytes 491528 | tf_op jit(solution)/shard_map/ppermute | solution.py:24
  28.1 3.8 %copy-start.1 = (bf16[1,128,640]{2,1,0:T(8,128)(2,1)S(1)}, bf16[1,128,640]{2,1,0:T(8,128)(2,1)}, u32[]{:S(2)}) copy-start(bf16[1,128,640]{2,1,0:T(8,128)(2,1)} %param.30) | copy-start | bytes 491524
  31.8 19.4 %copy-start.5 = (f32[30,640]{1,0:T(8,128)S(1)}, f32[30,640]{1,0:T(8,128)}, u32[]{:S(2)}) copy-start(f32[30,640]{1,0:T(8,128)} %param.35) | copy-start | bytes 230404
  31.9 19.4 %copy-start.6 = (s32[1,128]{1,0:T(1,128)S(1)}, s32[1,128]{1,0:T(1,128)}, u32[]{:S(2)}) copy-start(s32[1,128]{1,0:T(1,128)} %param.26) | copy-start | bytes 1540
  40.2 11.4 %copy-start.2 = (bf16[640,64]{0,1:T(8,128)(2,1)S(1)}, bf16[640,64]{0,1:T(8,128)(2,1)}, u32[]{:S(2)}) copy-start(bf16[640,64]{0,1:T(8,128)(2,1)} %param.36) | copy-start | bytes 245764
  47.7 20.2 %copy-start.3 = (f32[1,128,64]{1,2,0:T(8,128)S(1)}, f32[1,128,64]{1,2,0:T(8,128)}, u32[]{:S(2)}) copy-start(f32[1,128,64]{1,2,0:T(8,128)} %param.25) | copy-start | bytes 98308
  75.6 2.3 %collective-permute-start.1 = (bf16[2,4,64,16]{3,2,1,0:T(8,128)(2,1)S(1)}, bf16[2,4,64,16]{3,2,1,0:T(8,128)(2,1)S(1)}, u32[]{:S(2)}, u32[]{:S(2)}) collective-permute-start(bf16[2,4,64,16]{3,2,1,0:T(8,128)(2,1)S(1)} %bitcast.158), channel_id=1, source_target_pairs={{0,8},{8,16},{16,24},{1,9},{9,17},{17,25},{2,10},{10,18},{18,26},{... | collective-permute-start | bytes 49160 | tf_op jit(solution)/shard_map/ppermute | solution.py:24
  77.8 3.3 %collective-permute-start.2 = (bf16[4,4,1,16]{3,2,1,0:T(2,128)(2,1)S(1)}, bf16[4,4,1,16]{3,2,1,0:T(2,128)(2,1)S(1)}, u32[]{:S(2)}, u32[]{:S(2)}) collective-permute-start(bf16[4,4,1,16]{3,2,1,0:T(2,128)(2,1)S(1)} %get-tuple-element.221), channel_id=1, source_target_pairs={{0,4},{1,5},{2,6},{3,7},{8,12},{9,13},{10,14},{11,15},{16,20},{17,... | collective-permute-start | bytes 1544 | tf_op jit(solution)/shard_map/ppermute | solution.py:34
  79.8 5.5 %collective-permute-start.3 = (bf16[4,4,1,16]{3,2,1,0:T(2,128)(2,1)S(1)}, bf16[4,4,1,16]{3,2,1,0:T(2,128)(2,1)S(1)}, u32[]{:S(2)}, u32[]{:S(2)}) collective-permute-start(bf16[4,4,1,16]{3,2,1,0:T(2,128)(2,1)S(1)} %get-tuple-element.222), channel_id=1, source_target_pairs={{4,0},{5,1},{6,2},{7,3},{12,8},{13,9},{14,10},{15,11},{20,16},{21,... | collective-permute-start | bytes 1544 | tf_op jit(solution)/shard_map/ppermute | solution.py:35
  100.5 7.9 %copy-start.4 = (f32[96]{0:T(128)S(1)}, f32[96]{0:T(128)}, u32[]{:S(2)}) copy-start(f32[96]{0:T(128)} %param.38) | copy-start | bytes 1156
where the time goes:
time: 111 us; the launch traced here: 109 us
  blocking collectives  51.1 us (46%)
  local copies, waits for them, and re-layouts  31.5 us (28%)
  other arithmetic  9.69 us (9%)
  starting transfers between devices  6.87 us (6%)
  waiting for transfers between devices  5.21 us (5%)
  matrix products  3.19 us (3%)
  between operations  1.68 us (2%)
    unnamed x45, local copies, waits for them, and re-layouts  21.4 us
    psum x1, blocking collectives, body(): velocity = lax.psum(partial_sum, 'mp')  16.1 us
    psum x1, blocking collectives, body(): lax.psum((square_total(query_input[0]), square_total(key_input[0]), squar...  12.8 us
    all_gather x1, blocking collectives, body(): lax.all_gather(joint_values, 'seq', axis=0, tiled=True)  8.27 us
    all_gather x1, blocking collectives, body(): lax.all_gather(joint_keys, 'seq', axis=0, tiled=True)  7.5 us
    all_to_all x1, blocking collectives, body(): lax.all_to_all(rows_local, 'seq', split_axis=1, concat_axis=0, tiled=True)  6.44 us
    another operation x2, local copies, waits for them, and re-layouts, convolve(): jnp.stack(pieces, axis=3).reshape(frames_out * height * span_cols, 27 * LAT)  4.63 us
    ppermute x1, waiting for transfers between devices, padded_2(): after = lax.ppermute(initial, axis, down)  4.2 us
  transfers between devices with their start and end apart: 4, of which 2 were waited for; matrix products, arithmetic and copies ran while one was open for 8% of the time, Pallas kernels for 0%

commit v1 on v0

--- a/solution.py
+++ b/solution.py
@@ -4,6 +4,8 @@
 import jax.numpy as jnp
 import numpy as np
 from jax import lax
+from jax.experimental import pallas as pl
+from jax.experimental.pallas import tpu as pltpu
 from jax.sharding import PartitionSpec as P
 
 HEADS = 20
@@ -239,9 +241,405 @@
     return (next_latent[None], decoded[None])
 
 
+def wave_rows():
+    pairs_side = HD // 6
+    pairs_time = (HD - 4 * pairs_side) // 2
+    table = np.zeros((8, HD), np.float32)
+    for lane in range(HD):
+        pair = lane // 2
+        if pair < pairs_time:
+            table[0, lane] = np.float32(10000.0 ** (-pair / pairs_time))
+        elif pair < pairs_time + pairs_side:
+            table[1, lane] = np.float32(10000.0 ** (-(pair - pairs_time) / pairs_side))
+        else:
+            table[2, lane] = np.float32(10000.0 ** (-(pair - pairs_time - pairs_side) / pairs_side))
+            table[3, lane] = 1.0
+    return table
+
+
+MESH = pl.DeviceIdType.MESH
+F32 = jnp.float32
+BF16 = jnp.bfloat16
+NB, NS, NM = 4, 2, 4
+TOK, CTXR, WID, NH = 128, 64, 640, 5
+KEYS = TOK + CTXR
+
+
+def dot(a, b):
+    return lax.dot_general(a, b, (((1,), (0,)), ((), ())), preferred_element_type=F32)
+
+
+def dot_nt(a, b):
+    return lax.dot_general(a, b, (((1,), (1,)), ((), ())), preferred_element_type=F32)
+
+
+def dot_tn(a, b):
+    return lax.dot_general(a, b, (((0,), (0,)), ((), ())), preferred_element_type=F32)
+
+
+def step_kernel(
+    fo, noisy, step, q_in, k_in, v_in, ck_in, cv_in, qg, kg, gate, hw, cw, cb, waves,
+    next_out, dec_out,
+    qall, kbuf, vctx, ckrot, vt, wt, ebuf, numer, st_own, st_prev, dmine, dother, gatet,
+    part, rs, nl, lp, nz, sig_now, sig_step, wbig, fr, stage,
+    q_send, q_recv, c_send, c_recv, s_send, s_recv, sp_recv, d_send, d_recv,
+    r_send, r_recv, n_send, n_recv, l_send, l_recv,
+):
+    b = lax.axis_index("block")
+    s = lax.axis_index("seq")
+    m = lax.axis_index("mp")
+    nb = lax.rem(b + 1, NB)
+    pb = lax.rem(b + NB - 1, NB)
+    other = 1 - s
+
+    barrier = pltpu.get_barrier_semaphore()
+    for ds in range(NS):
+        for dm in range(NM):
+            ss, mm = lax.rem(s + ds, NS), lax.rem(m + dm, NM)
+            if ds or dm:
+                pl.semaphore_signal(barrier, inc=1, device_id=(b, ss, mm), device_id_type=MESH)
+            pl.semaphore_signal(barrier, inc=1, device_id=(pb, ss, mm), device_id_type=MESH)
+
+    lane = lax.broadcasted_iota(jnp.int32, (8, HD), 1)
+    even = lax.rem(lane, 2) == 0
+    sign = jnp.where(even, -1.0, 1.0)[0:1]
+    row8 = lax.broadcasted_iota(jnp.int32, (8, HD), 0)
+    base = fo[b]
+    tau = jnp.where(row8 == 2, base + 1, base + s).astype(F32)
+    hpos = jnp.where(row8 == 2, s, jnp.where(row8 == 1, 1, 0)).astype(F32)
+    ang = tau * waves[0:1] + hpos * waves[1:2]
+    cos_r, sin_r = jnp.cos(ang), jnp.sin(ang)
+    wpos = lax.broadcasted_iota(jnp.int32, (64, HD), 0).astype(F32)
+    ang_c = wpos * waves[2:3]
+    cos_c, sin_c = jnp.cos(ang_c), jnp.sin(ang_c)
+    col_lane = jnp.broadcast_to(waves[3:4], (64, HD)) > 0.5
+
+    def table(r):
+        c = jnp.where(col_lane, cos_c, jnp.broadcast_to(cos_r[r : r + 1], (64, HD)))
+        n = jnp.where(col_lane, sin_c, jnp.broadcast_to(sin_r[r : r + 1], (64, HD)))
+        return c, n * sign
+
+    c0, n0 = table(0)
+    c1, n1 = table(1)
+    cos_t = jnp.concatenate([c0, c1], 0)
+    sin_t = jnp.concatenate([n0, n1], 0)
+    cos_x, sin_x = table(2)
+
+    pr = lax.broadcasted_iota(jnp.int32, (HD, HD), 0)
+    pc = lax.broadcasted_iota(jnp.int32, (HD, HD), 1)
+    swap = jnp.where(pc == pr + 1 - 2 * lax.rem(pr, 2), 1.0, 0.0).astype(BF16)
+
+    def swapped(g):
+        g8 = jnp.broadcast_to(g, (8, HD))
+        return jnp.where(even, pltpu.roll(g8, HD - 1, 1), pltpu.roll(g8, 1, 1))[0:1]
+
+    def rotated(x_ref, gain, ct, st, store):
+        total = None
+        for h in range(NH):
+            sl = slice(h * HD, (h + 1) * HD)
+            xb = x_ref[0, :, sl]
+            x = xb.astype(F32)
+            g = gain[:, sl]
+            xs = dot(xb, swap)
+            store(sl, ((x * g) * ct + (xs * swapped(g)) * st).astype(BF16))
+            total = x * x if total is None else total + x * x
+        return total
+
+    def store_q(sl, val):
+        qall[s, :, sl] = val
+
+    def store_k(sl, val):
+        kbuf[0:TOK, sl] = val
+
+    def store_c(sl, val):
+        ckrot[:, sl] = val
+
+    sq_q = rotated(q_in, qg, cos_t, sin_t, store_q)
+    sq_c = rotated(ck_in, kg, cos_x, sin_x, store_c)
+    sq_k = rotated(k_in, kg, cos_t, sin_t, store_k)
+    row_q = jnp.sum(sq_q.T, axis=0, keepdims=True)
+    row_k = jnp.sum(sq_k.T, axis=0, keepdims=True)
+    sq_c2 = jnp.concatenate([sq_c, jnp.zeros((64, HD), F32)], 0)
+    row_c = jnp.sum(sq_c2.T, axis=0, keepdims=True)
+    step_row = step[...].astype(F32)
+    st_own[s, m] = jnp.where(
+        row8 == 0, row_q, jnp.where(row8 == 1, row_k, jnp.where(row8 == 2, row_c, step_row))
+    )
+
+    pl.semaphore_wait(barrier, 2 * NS * NM - 1)
+
+    def remote(src, dst, send, recv, dev):
+        return pltpu.make_async_remote_copy(
+            src_ref=src, dst_ref=dst, send_sem=send, recv_sem=recv, device_id=dev,
+            device_id_type=MESH,
+        )
+
+    pend = []
+
+    def go(*args):
+        copy = remote(*args)
+        copy.start()
+        pend.append(copy)
+
+    go(qall.at[s], qall.at[s], q_send, q_recv, (b, other, m))
+    go(ckrot, kbuf.at[pl.ds(TOK, CTXR)], c_send.at[0], c_recv.at[0], (nb, s, m))
+    go(cv_in.at[0], vctx, c_send.at[1], c_recv.at[1], (nb, s, m))
+    i = 0
+    for ds in range(NS):
+        for dm in range(NM):
+            ss, mm = lax.rem(s + ds, NS), lax.rem(m + dm, NM)
+            if ds or dm:
+                go(st_own.at[s, m], st_own.at[s, m], s_send.at[i], s_recv.at[s, m], (b, ss, mm))
+                i += 1
+    for dm in range(NM):
+        mm = lax.rem(m + dm, NM)
+        go(st_own.at[s, m], st_prev.at[m], s_send.at[i], sp_recv.at[m], (nb, s, mm))
+        i += 1
+
+    for h in range(NH):
+        sl = slice(h * HD, (h + 1) * HD)
+        vt[sl, 0:TOK] = v_in[0, :, sl].astype(F32).T.astype(BF16)
+        wt[:, sl] = hw[sl, :].astype(F32).T.astype(BF16)
+    steps_col = jnp.broadcast_to(step_row, (HD, HD)).T
+    lane64 = lax.broadcasted_iota(jnp.int32, (64, HD), 1)
+    steps2 = jnp.where(lane64 < 64, steps_col[0:64], steps_col[64:128])
+    nz[...] = jnp.concatenate([noisy[0, 0:64], noisy[0, 64:128]], 1)
+
+    def level(at):
+        remain = 1.0 - at / STEPS
+        return 8.0 * remain / (1.0 + 7.0 * remain)
+
+    now = level(steps2)
+    sig_now[...] = now
+    sig_step[...] = level(steps2 + 1.0) - now
+    lp[:, :, 0:16, :] = jnp.zeros((2, 2, 16, HD), BF16)
+    lp[:, :, 80:96, :] = jnp.zeros((2, 2, 16, HD), BF16)
+    wbig[...] = jnp.zeros(wbig.shape, BF16)
+    for qo in range(2):
+        for a in range(3):
+            for j in range(2):
+                for qi in range(2):
+                    d = qo + 2 * j + qi - 1
+                    if not 0 <= d <= 2:
+                        continue
+                    for y in range(4):
+                        for yo in range(4):
+                            t = y - yo + 1
+                            if not 0 <= t <= 2:
+                                continue
+                            r = a * 256 + j * 128 + y * 32 + qi * 16
+                            wbig[qo, r : r + 16, yo * 128 : yo * 128 + 96] = cw[a, t, d]
+
+    for ds in range(NS):
+        for dm in range(NM):
+            if ds or dm:
+                ss, mm = lax.rem(s + ds, NS), lax.rem(m + dm, NM)
+                remote(st_own.at[ss, mm], st_own.at[ss, mm], s_send.at[0], s_recv.at[ss, mm],
+                       (b, other, m)).wait_recv()
+    for mm in range(NM):
+        remote(st_prev.at[mm], st_prev.at[mm], s_send.at[0], sp_recv.at[mm],
+               (b, other, m)).wait_recv()
+    inv = 1.0 / (HEADS * HD)
+    qstat = [st_own[e, 0] + st_own[e, 1] + st_own[e, 2] + st_own[e, 3] for e in range(NS)]
+    kstat = st_own[s, 0] + st_own[s, 1] + st_own[s, 2] + st_own[s, 3]
+    cstat = st_prev[0] + st_prev[1] + st_prev[2] + st_prev[3]
+    scale = 1.4426950408889634 / math.sqrt(HD)
+    fq = [lax.rsqrt(x[0:1] * inv + 1e-06) * scale for x in qstat]
+    fk_own = jnp.broadcast_to(lax.rsqrt(kstat[1:2] * inv + 1e-06), (HD, HD)).T
+    fk_ctx = jnp.broadcast_to(lax.rsqrt(cstat[2:3] * inv + 1e-06), (HD, HD)).T[0:CTXR]
+    fk = jnp.concatenate([fk_own, fk_ctx], 0)
+    factor = jnp.concatenate([fk * fq[0], fk * fq[1]], 1)
+
+    steps_all = jnp.concatenate([st_own[0, 0][3:4], st_own[1, 0][3:4]], 1)
+    which = lax.broadcasted_iota(jnp.int32, (STEPS, 2 * TOK), 0).astype(F32)
+    hot = jnp.where(which == steps_all, 1.0, 0.0).astype(BF16)
+    g_all = gate[...]
+    g_hi = g_all.astype(BF16)
+    g_lo = (g_all - g_hi.astype(F32)).astype(BF16)
+    gatet[...] = dot_tn(g_hi, hot) + dot_tn(g_lo, hot)
+
+    remote(ckrot, kbuf.at[pl.ds(TOK, CTXR)], c_send.at[0], c_recv.at[0], (b, other, m)).wait_recv()
+    remote(vctx, vctx, c_send.at[1], c_recv.at[1], (b, other, m)).wait_recv()
+    for h in range(NH):
+        sl = slice(h * HD, (h + 1) * HD)
+        vt[sl, TOK:KEYS] = vctx[:, sl].astype(F32).T.astype(BF16)
+    remote(qall.at[other], qall.at[other], q_send, q_recv, (b, other, m)).wait_recv()
+
+    has_prior = jnp.broadcast_to(b, (CTXR, 2 * TOK)) > 0
+    sub = lax.broadcasted_iota(jnp.int32, (8, 2 * TOK), 0)
+    sums = jnp.ones((8, 2 * TOK), F32)
+    for h in range(NH):
+        sl = slice(h * HD, (h + 1) * HD)
+        qh = jnp.concatenate([qall[0, :, sl], qall[1, :, sl]], 0)
+        sc = dot_nt(kbuf[:, sl], qh) * factor
+        e = jnp.exp2(sc)
+        e_own = e[0:TOK]
+        e_ctx = jnp.where(has_prior, e[TOK:KEYS], 0.0)
+        den = jnp.sum(e_own, axis=0, keepdims=True) + jnp.sum(e_ctx, axis=0, keepdims=True)
+        sums = jnp.where(sub == h, den, sums)
+        ebuf[h, 0:TOK] = e_own.astype(BF16)
+        ebuf[h, TOK:KEYS] = e_ctx.astype(BF16)
+    dmine[...] = sums
+    go(dmine, dother, d_send, d_recv, (b, other, m))
+    for h in range(NH):
+        sl = slice(h * HD, (h + 1) * HD)
+        numer[sl] = dot(vt[sl, :], ebuf[h]) * gatet[sl]
+    remote(dmine, dother, d_send, d_recv, (b, other, m)).wait_recv()
+    recip = 1.0 / (dmine[...] + dother[...])
+    vel_t = jnp.zeros((64, 2 * TOK), F32)
+    for h in range(NH):
+        sl = slice(h * HD, (h + 1) * HD)
+        vel_t += dot(wt[:, sl], (numer[sl] * recip[h : h + 1]).astype(BF16))
+    for f in range(2):
+        t = jnp.concatenate([vel_t[:, f * TOK : (f + 1) * TOK], jnp.zeros((64, HD), F32)], 0).T
+        part[f] = jnp.concatenate([t[0:64, 0:64], t[64:128, 0:64]], 1)
+
+    def cols(mm):
+        return pl.ds(pl.multiple_of(mm * 16, 16), 16)
+
+    def lcols(mm):
+        return pl.ds(pl.multiple_of(mm * 16 + 16, 16), 16)
+
+    i = 0
+    for ds in range(NS):
+        for dm in range(NM):
+            if ds or dm:
+                ss, mm = lax.rem(s + ds, NS), lax.rem(m + dm, NM)
+                go(part.at[ss, cols(mm)], rs.at[s, m], r_send.at[i], r_recv.at[s, m], (b, ss, mm))
+                i += 1
+    rs[s, m] = part[s, cols(m)]
+    for ds in range(NS):
+        for dm in range(NM):
+            if ds or dm:
+                ss, mm = lax.rem(s + ds, NS), lax.rem(m + dm, NM)
+                remote(rs.at[ss, mm], rs.at[ss, mm], r_send.at[0], r_recv.at[ss, mm],
+                       (b, other, m)).wait_recv()
+    vel = rs[0, 0]
+    for e in range(1, NS * NM):
+        vel = vel + rs[e // NM, e % NM]
+    latent = nz[cols(m), :]
+    lp[1, s, lcols(m), :] = (latent - sig_now[cols(m), :] * vel).astype(BF16)
+    mine = lp.at[1, s, lcols(m)]
+    i = 0
+    for ds in range(NS):
+        for dm in range(NM):
+            ss, mm = lax.rem(s + ds, NS), lax.rem(m + dm, NM)
+            go(mine, lp.at[0, s, lcols(m)], l_send.at[i], l_recv.at[0, s, m], (nb, ss, mm))
+            i += 1
+            if ds or dm:
+                go(mine, mine, l_send.at[i], l_recv.at[1, s, m], (b, ss, mm))
+                i += 1
+    nl[cols(m), :] = latent + sig_step[cols(m), :] * vel
+    for dm in range(1, NM):
+        mm = lax.rem(m + dm, NM)
+        go(nl.at[cols(m)], nl.at[cols(m)], n_send.at[dm - 1], n_recv.at[m], (b, s, mm))
+
+    for c in (1, 0):
+        for ds in range(NS):
+            for dm in range(NM):
+                if c == 0 or ds or dm:
+                    ss, mm = lax.rem(s + ds, NS), lax.rem(m + dm, NM)
+                    at = lp.at[c, ss, lcols(mm)]
+                    remote(at, at, l_send.at[0], l_recv.at[c, ss, mm], (b, other, m)).wait_recv()
+    slab = pl.ds(pl.multiple_of(s * 32, 32), 64)
+    prior2 = jnp.broadcast_to(b, (64, HD)) > 0
+    for f in range(2):
+        fr[f] = jnp.where(prior2, lp[0, f, slab, :].astype(F32), 0.0)
+        fr[2 + f] = lp[1, f, slab, :].astype(F32)
+    bias = cb[...]
+    for qo in range(2):
+        rows = []
+        for t in range(2):
+            taps = []
+            for a in range(3):
+                for j in range(2):
+                    taps.append(fr[t + a, 15 + qo + j : 47 + qo + j, :].astype(BF16))
+            rows.append(jnp.concatenate(taps, 1))
+        res = dot(jnp.concatenate(rows, 0), wbig[qo])
+        for t in range(2):
+            for y in range(4):
+                stage[t * 4 + y, pl.ds(qo, 32, stride=2), :] = res[
+                    t * 32 : (t + 1) * 32, y * 128 : (y + 1) * 128
+                ]
+    for t in range(2):
+        for y in range(4):
+            dec_out[0, t, y] = (stage[t * 4 + y][:, 0:96] + bias).astype(BF16)
+
+    for dm in range(1, NM):
+        mm = lax.rem(m + dm, NM)
+        remote(nl.at[cols(mm)], nl.at[cols(mm)], n_send.at[0], n_recv.at[mm],
+               (b, other, m)).wait_recv()
+    final = nl[...]
+    next_out[0, 0:64] = final[:, 0:64]
+    next_out[0, 64:128] = final[:, 64:128]
+    for copy in pend:
+        copy.wait_send()
+
+
+def fused_body(
+    noisy_latent, step_index, frame_offset, query_input, key_input, value_input, context_keys,
+    context_values, query_gain, key_gain, gate_table, head_weight, conv_weight, conv_bias,
+):
+    vmem = pl.BlockSpec(memory_space=pltpu.VMEM)
+    dma = pltpu.SemaphoreType.DMA
+    scratch = [
+        pltpu.VMEM((2, TOK, WID), BF16),
+        pltpu.VMEM((KEYS, WID), BF16),
+        pltpu.VMEM((CTXR, WID), BF16),
+        pltpu.VMEM((CTXR, WID), BF16),
+        pltpu.VMEM((WID, KEYS), BF16),
+        pltpu.VMEM((64, WID), BF16),
+        pltpu.VMEM((NH, KEYS, 2 * TOK), BF16),
+        pltpu.VMEM((WID, 2 * TOK), F32),
+        pltpu.VMEM((NS, NM, 8, HD), F32),
+        pltpu.VMEM((NM, 8, HD), F32),
+        pltpu.VMEM((8, 2 * TOK), F32),
+        pltpu.VMEM((8, 2 * TOK), F32),
+        pltpu.VMEM((WID, 2 * TOK), F32),
+        pltpu.VMEM((2, 64, HD), F32),
+        pltpu.VMEM((NS, NM, 16, HD), F32),
+        pltpu.VMEM((64, HD), F32),
+        pltpu.VMEM((2, 2, 96, HD), BF16),
+        pltpu.VMEM((64, HD), F32),
+        pltpu.VMEM((64, HD), F32),
+        pltpu.VMEM((64, HD), F32),
+        pltpu.VMEM((2, 768, 512), BF16),
+        pltpu.VMEM((4, 64, HD), F32),
+        pltpu.VMEM((8, 64, HD), F32),
+        dma, dma, dma((2,)), dma((2,)),
+        dma((11,)), dma((NS, NM)), dma((NM,)),
+        dma, dma,
+        dma((7,)), dma((NS, NM)),
+        dma((3,)), dma((NM,)),
+        dma((15,)), dma((2, NS, NM)),
+    ]
+    return pl.pallas_call(
+        step_kernel,
+        out_shape=(
+            jax.ShapeDtypeStruct((1, TOK, 64), F32),
+            jax.ShapeDtypeStruct((1, 2, 4, 64, 96), BF16),
+        ),
+        in_specs=[pl.BlockSpec(memory_space=pltpu.SMEM)] + [vmem] * 14,
+        out_specs=(vmem, vmem),
+        scratch_shapes=scratch,
+        compiler_params=pltpu.CompilerParams(
+            collective_id=0, has_side_effects=True, vmem_limit_bytes=32 * 1024 * 1024
+        ),
+    )(
+        frame_offset, noisy_latent, step_index, query_input, key_input, value_input,
+        context_keys, context_values, query_gain.reshape(1, -1), key_gain.reshape(1, -1),
+        gate_table, head_weight, conv_weight, conv_bias.reshape(1, -1),
+        jnp.asarray(wave_rows()),
+    )
+
+
+def fused_fits(mesh):
+    return dict(mesh.shape) == {"block": NB, "seq": NS, "mp": NM}
+
+
 def solution(mesh):
     return jax.shard_map(
-        body,
+        fused_body if fused_fits(mesh) else body,
         mesh=mesh,
         in_specs=(
             P("block", "seq", None),

time: 111 us -> 36.8 us (0.33); the launches traced: 109 us -> 36.4 us
  blocking collectives: 51.1 us -> 0 us
  Pallas kernels: 0 us -> 27.1 us
  local copies, waits for them, and re-layouts: 31.5 us -> 8.52 us
  other arithmetic: 9.69 us -> 0 us
  starting transfers between devices: 6.87 us -> 0 us
  waiting for transfers between devices: 5.21 us -> 0 us
  matrix products: 3.19 us -> 0 us
    psum x2 -> x0, blocking collectives: 28.9 us -> none  [the longest x1 16.1 us: body(): velocity = lax.psum(partial_sum, 'mp')]
    pallas_call x0 -> x1, Pallas kernels: none -> 27.1 us  [fused_body(): pl.pallas_call(step_kernel, out_shape=(jax.ShapeDtypeStruct((1, TOK, 64),...]
    all_gather x2 -> x0, blocking collectives: 15.8 us -> none  [the longest x1 8.27 us: body(): lax.all_gather(joint_values, 'seq', axis=0, tiled=True)]
    unnamed x45 -> x27, local copies, waits for them, and re-layouts: 21.4 us -> 7.12 us
    ppermute x4 -> x0, starting transfers between devices: 6.87 us -> none  [the longest x2 3.67 us: passed_along(): return lax.ppermute(x, axis, pairs)]
    all_to_all x1 -> x0, blocking collectives: 6.44 us -> none  [body(): lax.all_to_all(rows_local, 'seq', split_axis=1, concat_axis=0, tiled=True)]
    ppermute x4 -> x0, waiting for transfers between devices: 5.21 us -> none  [the longest x1 4.2 us: padded_2(): after = lax.ppermute(initial, axis, down)]
    another operation x2 -> x0, local copies, waits for them, and re-layouts: 4.63 us -> none  [convolve(): jnp.stack(pieces, axis=3).reshape(frames_out * height * span_cols, 27 * LAT)]
  transfers between devices with their start and end apart: 4 -> 0, of which waited for: 2 -> 0; matrix products, arithmetic and copies ran while one was open for 8% -> 0% of each run, Pallas kernels for 0% -> 0%
where the time goes in v1:
time: 36.8 us; the launch traced here: 36.4 us
  Pallas kernels  27.1 us (74%)
  local copies, waits for them, and re-layouts  8.52 us (23%)
  between operations  0.76 us (2%)
    pallas_call x1, Pallas kernels, fused_body(): pl.pallas_call(step_kernel, out_shape=(jax.ShapeDtypeStruct((1, TOK, 64),...  27.1 us
    unnamed x27, local copies, waits for them, and re-layouts  7.12 us

profile of v1, /device:TPU:0, one launch (start us, length us, event | category | flops | bytes accessed | tf_op | source)
XLA Modules:
  0.0 36.4 jit_solution(2133650196651557907)
XLA Ops:
  0.6 0.0 copy-start.11
  0.6 0.7 %reshape.13.qg = f32[1,640]{1,0:T(1,128)S(1)} reshape(f32[640]{0:T(1024)} %param.23) | data formatting | bytes 5120 | tf_op jit(solution)/shard_map/reshape | solution.py:630
  1.3 0.0 copy-done.11
  1.3 0.0 copy-start
  1.3 0.0 copy-start.1
  1.4 0.9 %copy.17.noisy = f32[1,128,64]{2,1,0:T(8,128)S(1)} copy(f32[1,128,64]{1,2,0:T(8,128)} %param.15) | data formatting | bytes 65536 | tf_op args[0]
  2.3 0.0 copy-start.7
  2.3 0.0 copy-start.8
  2.3 0.0 copy-start.9
  2.3 0.0 copy-start.10
  2.3 1.1 %copy.18.hw = bf16[640,64]{1,0:T(8,128)(2,1)S(1)} copy(bf16[640,64]{0,1:T(8,128)(2,1)} %param.26) | data formatting | bytes 163840 | tf_op args[11]
  3.4 0.0 copy-done
  3.4 0.0 copy-done.1
  3.4 0.0 copy-done.7
  3.4 0.0 copy-done.8
  3.4 0.0 copy-done.9
  3.4 0.0 copy-done.10
  3.4 0.0 copy-start.2
  3.4 0.9 %copy-done.2 = bf16[1,128,640]{2,1,0:T(8,128)(2,1)S(1)} copy-done((bf16[1,128,640]{2,1,0:T(8,128)(2,1)S(1)}, bf16[1,128,640]{2,1,0:T(8,128)(2,1)}, u32[]{:S(2)}) %copy-start.2) | copy-done | bytes 163864
  4.4 0.0 copy-start.3
  4.4 0.9 %copy-done.3 = bf16[3,3,3,16,96]{4,3,2,1,0:T(8,128)(2,1)S(1)} copy-done((bf16[3,3,3,16,96]{4,3,2,1,0:T(8,128)(2,1)S(1)}, bf16[3,3,3,16,96]{4,3,2,1,0:T(8,128)(2,1)}, u32[]{:S(2)}) %copy-start.3) | copy-done | bytes 82968
  5.3 0.0 copy-start.4
  5.3 0.9 %copy-done.4 = bf16[1,64,640]{2,1,0:T(8,128)(2,1)S(1)} copy-done((bf16[1,64,640]{2,1,0:T(8,128)(2,1)S(1)}, bf16[1,64,640]{2,1,0:T(8,128)(2,1)}, u32[]{:S(2)}) %copy-start.4) | copy-done | bytes 81944
  6.1 0.0 copy-start.5
  6.1 0.9 %copy-done.5 = bf16[1,64,640]{2,1,0:T(8,128)(2,1)S(1)} copy-done((bf16[1,64,640]{2,1,0:T(8,128)(2,1)S(1)}, bf16[1,64,640]{2,1,0:T(8,128)(2,1)}, u32[]{:S(2)}) %copy-start.5) | copy-done | bytes 81944
  7.0 0.0 copy-start.6
  7.0 0.9 %copy-done.6 = f32[30,640]{1,0:T(8,128)S(1)} copy-done((f32[30,640]{1,0:T(8,128)S(1)}, f32[30,640]{1,0:T(8,128)}, u32[]{:S(2)}) %copy-start.6) | copy-done | bytes 76824
  7.9 27.1 %shard_map.158 = (f32[1,128,64]{2,1,0:T(8,128)S(1)}, bf16[1,2,4,64,96]{4,3,2,1,0:T(8,128)(2,1)S(1)}) custom-call(s32[4]{0:T(128)S(1)} %copy-done.8, f32[1,128,64]{2,1,0:T(8,128)S(1)} %copy.17.noisy, s32[1,128]{1,0:T(1,128)S(1)} %copy-done.9, bf16[1,128,640]{2,1,0:T(8,128)(2,1)S(1)} %copy-done, bf16[1,128,640]{2,1,0:T(8,128)(2,1)S(1)} %copy-done.1, ...), custom_call_target="tpu_custom_call" | custom-call | tf_op jit(solution)/shard_map/pallas_call | solution.py:616
  35.1 0.7 %copy.19 = f32[1,128,64]{1,2,0:T(8,128)} copy(f32[1,128,64]{2,1,0:T(8,128)S(1)} %get-tuple-element.2) | data formatting | bytes 65536 | tf_op jit(solution)/shard_map/pallas_call | solution.py:616
  35.8 0.7 %copy.21 = bf16[1,2,4,64,96]{4,3,2,1,0:T(8,128)(2,1)} copy(bf16[1,2,4,64,96]{4,3,2,1,0:T(8,128)(2,1)S(1)} %get-tuple-element.7) | data formatting | bytes 196608
  (1 shorter events, 0.0 us)
Async XLA Ops:
  0.6 0.7 %copy-start.11 = (f32[640]{0:T(1024)S(1)}, f32[640]{0:T(1024)}, u32[]{:S(2)}) copy-start(f32[640]{0:T(1024)} %param.24) | copy-start | bytes 7684
  1.3 2.0 %copy-start = (bf16[1,128,640]{2,1,0:T(8,128)(2,1)S(1)}, bf16[1,128,640]{2,1,0:T(8,128)(2,1)}, u32[]{:S(2)}) copy-start(bf16[1,128,640]{2,1,0:T(8,128)(2,1)} %q_in.1) | copy-start | bytes 491524
  1.3 2.0 %copy-start.1 = (bf16[1,128,640]{2,1,0:T(8,128)(2,1)S(1)}, bf16[1,128,640]{2,1,0:T(8,128)(2,1)}, u32[]{:S(2)}) copy-start(bf16[1,128,640]{2,1,0:T(8,128)(2,1)} %k_in.1) | copy-start | bytes 491524
  2.3 1.1 %copy-start.7 = (f32[8,128]{1,0:T(8,128)S(1)}, f32[8,128]{1,0:T(8,128)}, u32[]{:S(2)}) copy-start(f32[8,128]{1,0:T(8,128)} %constant.2.clone.waves) | copy-start | bytes 12292
  2.3 1.1 %copy-start.8 = (s32[4]{0:T(128)S(1)}, s32[4]{0:T(128)}, u32[]{:S(2)}) copy-start(s32[4]{0:T(128)} %fo.1) | copy-start | bytes 52
  2.3 1.1 %copy-start.9 = (s32[1,128]{1,0:T(1,128)S(1)}, s32[1,128]{1,0:T(1,128)}, u32[]{:S(2)}) copy-start(s32[1,128]{1,0:T(1,128)} %step.1) | copy-start | bytes 1540
  2.3 1.1 %copy-start.10 = (f32[96]{0:T(128)S(1)}, f32[96]{0:T(128)}, u32[]{:S(2)}) copy-start(f32[96]{0:T(128)} %param.28) | copy-start | bytes 1156
  3.4 0.9 %copy-start.2 = (bf16[1,128,640]{2,1,0:T(8,128)(2,1)S(1)}, bf16[1,128,640]{2,1,0:T(8,128)(2,1)}, u32[]{:S(2)}) copy-start(bf16[1,128,640]{2,1,0:T(8,128)(2,1)} %v_in.1) | copy-start | bytes 491524
  4.4 0.9 %copy-start.3 = (bf16[3,3,3,16,96]{4,3,2,1,0:T(8,128)(2,1)S(1)}, bf16[3,3,3,16,96]{4,3,2,1,0:T(8,128)(2,1)}, u32[]{:S(2)}) copy-start(bf16[3,3,3,16,96]{4,3,2,1,0:T(8,128)(2,1)} %cw.1) | copy-start | bytes 248836
  5.3 0.9 %copy-start.4 = (bf16[1,64,640]{2,1,0:T(8,128)(2,1)S(1)}, bf16[1,64,640]{2,1,0:T(8,128)(2,1)}, u32[]{:S(2)}) copy-start(bf16[1,64,640]{2,1,0:T(8,128)(2,1)} %ck_in.1) | copy-start | bytes 245764
  6.1 0.9 %copy-start.5 = (bf16[1,64,640]{2,1,0:T(8,128)(2,1)S(1)}, bf16[1,64,640]{2,1,0:T(8,128)(2,1)}, u32[]{:S(2)}) copy-start(bf16[1,64,640]{2,1,0:T(8,128)(2,1)} %cv_in.1) | copy-start | bytes 245764
  7.0 0.9 %copy-start.6 = (f32[30,640]{1,0:T(8,128)S(1)}, f32[30,640]{1,0:T(8,128)}, u32[]{:S(2)}) copy-start(f32[30,640]{1,0:T(8,128)} %gate.1) | copy-start | bytes 230404

commit v2 on v1

--- a/solution.py
+++ b/solution.py
@@ -278,9 +278,11 @@
 
 
 def step_kernel(
-    fo, noisy, step, q_in, k_in, v_in, ck_in, cv_in, qg, kg, gate, hw, cw, cb, waves,
+    fo_hbm, noisy_hbm, step_hbm, q_hbm, k_hbm, v_hbm, ck_hbm, cv_hbm, qg_hbm, kg_hbm, gate_hbm,
+    hw_hbm, cw_hbm, cb_hbm, waves_hbm,
     next_out, dec_out,
-    qall, kbuf, vctx, ckrot, vt, wt, ebuf, numer, st_own, st_prev, dmine, dother, gatet,
+    fo, noisy, step, q_in, k_in, v_in, ck_in, qg, kg, gate, wt, cw, cb, waves, in_sem,
+    qall, kbuf, vctx, ckrot, vt, ebuf, numer, st_own, st_prev, dmine, dother, gatet,
     part, rs, nl, lp, nz, sig_now, sig_step, wbig, fr, stage,
     q_send, q_recv, c_send, c_recv, s_send, s_recv, sp_recv, d_send, d_recv,
     r_send, r_recv, n_send, n_recv, l_send, l_recv,
@@ -300,10 +302,22 @@
                 pl.semaphore_signal(barrier, inc=1, device_id=(b, ss, mm), device_id_type=MESH)
             pl.semaphore_signal(barrier, inc=1, device_id=(pb, ss, mm), device_id_type=MESH)
 
+    loads = {}
+    for i, (name, src, dst) in enumerate((
+        ("fo", fo_hbm, fo), ("waves", waves_hbm, waves), ("q", q_hbm, q_in), ("qg", qg_hbm, qg),
+        ("ck", ck_hbm, ck_in), ("kg", kg_hbm, kg), ("k", k_hbm, k_in), ("step", step_hbm, step),
+        ("v", v_hbm, v_in), ("cw", cw_hbm, cw), ("gate", gate_hbm, gate), ("wt", hw_hbm, wt),
+        ("noisy", noisy_hbm, noisy), ("cb", cb_hbm, cb),
+    )):
+        loads[name] = pltpu.make_async_copy(src, dst, in_sem.at[i])
+        loads[name].start()
+
     lane = lax.broadcasted_iota(jnp.int32, (8, HD), 1)
     even = lax.rem(lane, 2) == 0
     sign = jnp.where(even, -1.0, 1.0)[0:1]
     row8 = lax.broadcasted_iota(jnp.int32, (8, HD), 0)
+    loads["fo"].wait()
+    loads["waves"].wait()
     base = fo[b]
     tau = jnp.where(row8 == 2, base + 1, base + s).astype(F32)
     hpos = jnp.where(row8 == 2, s, jnp.where(row8 == 1, 1, 0)).astype(F32)
@@ -339,7 +353,7 @@
             sl = slice(h * HD, (h + 1) * HD)
             xb = x_ref[0, :, sl]
             x = xb.astype(F32)
-            g = gain[:, sl]
+            g = gain[h : h + 1]
             xs = dot(xb, swap)
             store(sl, ((x * g) * ct + (xs * swapped(g)) * st).astype(BF16))
             total = x * x if total is None else total + x * x
@@ -354,13 +368,19 @@
     def store_c(sl, val):
         ckrot[:, sl] = val
 
+    loads["q"].wait()
+    loads["qg"].wait()
     sq_q = rotated(q_in, qg, cos_t, sin_t, store_q)
+    loads["ck"].wait()
+    loads["kg"].wait()
     sq_c = rotated(ck_in, kg, cos_x, sin_x, store_c)
+    loads["k"].wait()
     sq_k = rotated(k_in, kg, cos_t, sin_t, store_k)
     row_q = jnp.sum(sq_q.T, axis=0, keepdims=True)
     row_k = jnp.sum(sq_k.T, axis=0, keepdims=True)
     sq_c2 = jnp.concatenate([sq_c, jnp.zeros((64, HD), F32)], 0)
     row_c = jnp.sum(sq_c2.T, axis=0, keepdims=True)
+    loads["step"].wait()
     step_row = step[...].astype(F32)
     st_own[s, m] = jnp.where(
         row8 == 0, row_q, jnp.where(row8 == 1, row_k, jnp.where(row8 == 2, row_c, step_row))
@@ -381,9 +401,6 @@
         copy.start()
         pend.append(copy)
 
-    go(qall.at[s], qall.at[s], q_send, q_recv, (b, other, m))
-    go(ckrot, kbuf.at[pl.ds(TOK, CTXR)], c_send.at[0], c_recv.at[0], (nb, s, m))
-    go(cv_in.at[0], vctx, c_send.at[1], c_recv.at[1], (nb, s, m))
     i = 0
     for ds in range(NS):
         for dm in range(NM):
@@ -397,13 +414,21 @@
         i += 1
 
     for h in range(NH):
+        hl = pl.ds(h * HD, HD)
+        go(qall.at[s, :, hl], qall.at[s, :, hl], q_send.at[h], q_recv.at[h], (b, other, m))
+        go(ckrot.at[:, hl], kbuf.at[pl.ds(TOK, CTXR), hl], c_send.at[h], c_recv.at[h], (nb, s, m))
+    go(cv_hbm.at[0], vctx, c_send.at[NH], c_recv.at[NH], (nb, s, m))
+
+    loads["v"].wait()
+    for h in range(NH):
         sl = slice(h * HD, (h + 1) * HD)
         vt[sl, 0:TOK] = v_in[0, :, sl].astype(F32).T.astype(BF16)
-        wt[:, sl] = hw[sl, :].astype(F32).T.astype(BF16)
     steps_col = jnp.broadcast_to(step_row, (HD, HD)).T
     lane64 = lax.broadcasted_iota(jnp.int32, (64, HD), 1)
     steps2 = jnp.where(lane64 < 64, steps_col[0:64], steps_col[64:128])
-    nz[...] = jnp.concatenate([noisy[0, 0:64], noisy[0, 64:128]], 1)
+    loads["noisy"].wait()
+    t = jnp.concatenate([noisy[0], jnp.zeros((64, HD), F32)], 0).T
+    nz[...] = jnp.concatenate([t[0:64, 0:64], t[64:128, 0:64]], 1)
 
     def level(at):
         remain = 1.0 - at / STEPS
@@ -415,6 +440,7 @@
     lp[:, :, 0:16, :] = jnp.zeros((2, 2, 16, HD), BF16)
     lp[:, :, 80:96, :] = jnp.zeros((2, 2, 16, HD), BF16)
     wbig[...] = jnp.zeros(wbig.shape, BF16)
+    loads["cw"].wait()
     for qo in range(2):
         for a in range(3):
             for j in range(2):
@@ -453,23 +479,22 @@
     steps_all = jnp.concatenate([st_own[0, 0][3:4], st_own[1, 0][3:4]], 1)
     which = lax.broadcasted_iota(jnp.int32, (STEPS, 2 * TOK), 0).astype(F32)
     hot = jnp.where(which == steps_all, 1.0, 0.0).astype(BF16)
+    loads["gate"].wait()
     g_all = gate[...]
     g_hi = g_all.astype(BF16)
     g_lo = (g_all - g_hi.astype(F32)).astype(BF16)
     gatet[...] = dot_tn(g_hi, hot) + dot_tn(g_lo, hot)
-
-    remote(ckrot, kbuf.at[pl.ds(TOK, CTXR)], c_send.at[0], c_recv.at[0], (b, other, m)).wait_recv()
-    remote(vctx, vctx, c_send.at[1], c_recv.at[1], (b, other, m)).wait_recv()
-    for h in range(NH):
-        sl = slice(h * HD, (h + 1) * HD)
-        vt[sl, TOK:KEYS] = vctx[:, sl].astype(F32).T.astype(BF16)
-    remote(qall.at[other], qall.at[other], q_send, q_recv, (b, other, m)).wait_recv()
 
     has_prior = jnp.broadcast_to(b, (CTXR, 2 * TOK)) > 0
     sub = lax.broadcasted_iota(jnp.int32, (8, 2 * TOK), 0)
     sums = jnp.ones((8, 2 * TOK), F32)
     for h in range(NH):
         sl = slice(h * HD, (h + 1) * HD)
+        hl = pl.ds(h * HD, HD)
+        remote(qall.at[s, :, hl], qall.at[other, :, hl], q_send.at[h], q_recv.at[h],
+               (b, other, m)).wait_recv()
+        remote(ckrot.at[:, hl], kbuf.at[pl.ds(TOK, CTXR), hl], c_send.at[h], c_recv.at[h],
+               (b, other, m)).wait_recv()
         qh = jnp.concatenate([qall[0, :, sl], qall[1, :, sl]], 0)
         sc = dot_nt(kbuf[:, sl], qh) * factor
         e = jnp.exp2(sc)
@@ -481,11 +506,16 @@
         ebuf[h, TOK:KEYS] = e_ctx.astype(BF16)
     dmine[...] = sums
     go(dmine, dother, d_send, d_recv, (b, other, m))
+    remote(vctx, vctx, c_send.at[NH], c_recv.at[NH], (b, other, m)).wait_recv()
+    for h in range(NH):
+        sl = slice(h * HD, (h + 1) * HD)
+        vt[sl, TOK:KEYS] = vctx[:, sl].astype(F32).T.astype(BF16)
     for h in range(NH):
         sl = slice(h * HD, (h + 1) * HD)
         numer[sl] = dot(vt[sl, :], ebuf[h]) * gatet[sl]
     remote(dmine, dother, d_send, d_recv, (b, other, m)).wait_recv()
     recip = 1.0 / (dmine[...] + dother[...])
+    loads["wt"].wait()
     vel_t = jnp.zeros((64, 2 * TOK), F32)
     for h in range(NH):
         sl = slice(h * HD, (h + 1) * HD)
@@ -546,6 +576,7 @@
     for f in range(2):
         fr[f] = jnp.where(prior2, lp[0, f, slab, :].astype(F32), 0.0)
         fr[2 + f] = lp[1, f, slab, :].astype(F32)
+    loads["cb"].wait()
     bias = cb[...]
     for qo in range(2):
         rows = []
@@ -569,9 +600,8 @@
         mm = lax.rem(m + dm, NM)
         remote(nl.at[cols(mm)], nl.at[cols(mm)], n_send.at[0], n_recv.at[mm],
                (b, other, m)).wait_recv()
-    final = nl[...]
-    next_out[0, 0:64] = final[:, 0:64]
-    next_out[0, 64:128] = final[:, 64:128]
+    final = jnp.concatenate([nl[...], jnp.zeros((64, HD), F32)], 0).T
+    next_out[0] = jnp.concatenate([final[0:64, 0:64], final[64:128, 0:64]], 1)
     for copy in pend:
         copy.wait_send()
 
@@ -583,12 +613,26 @@
     vmem = pl.BlockSpec(memory_space=pltpu.VMEM)
     dma = pltpu.SemaphoreType.DMA
     scratch = [
+        pltpu.SMEM((4,), jnp.int32),
+        pltpu.VMEM((1, 64, TOK), F32),
+        pltpu.VMEM((1, TOK), jnp.int32),
+        pltpu.VMEM((1, TOK, WID), BF16),
+        pltpu.VMEM((1, TOK, WID), BF16),
+        pltpu.VMEM((1, TOK, WID), BF16),
+        pltpu.VMEM((1, CTXR, WID), BF16),
+        pltpu.VMEM((NH, HD), F32),
+        pltpu.VMEM((NH, HD), F32),
+        pltpu.VMEM((STEPS, WID), F32),
+        pltpu.VMEM((64, WID), BF16),
+        pltpu.VMEM((3, 3, 3, LAT, 96), BF16),
+        pltpu.VMEM((1, 96), F32),
+        pltpu.VMEM((8, HD), F32),
+        dma((14,)),
         pltpu.VMEM((2, TOK, WID), BF16),
         pltpu.VMEM((KEYS, WID), BF16),
         pltpu.VMEM((CTXR, WID), BF16),
         pltpu.VMEM((CTXR, WID), BF16),
         pltpu.VMEM((WID, KEYS), BF16),
-        pltpu.VMEM((64, WID), BF16),
         pltpu.VMEM((NH, KEYS, 2 * TOK), BF16),
         pltpu.VMEM((WID, 2 * TOK), F32),
         pltpu.VMEM((NS, NM, 8, HD), F32),
@@ -606,31 +650,33 @@
         pltpu.VMEM((2, 768, 512), BF16),
         pltpu.VMEM((4, 64, HD), F32),
         pltpu.VMEM((8, 64, HD), F32),
-        dma, dma, dma((2,)), dma((2,)),
+        dma((NH,)), dma((NH,)), dma((NH + 1,)), dma((NH + 1,)),
         dma((11,)), dma((NS, NM)), dma((NM,)),
         dma, dma,
         dma((7,)), dma((NS, NM)),
         dma((3,)), dma((NM,)),
         dma((15,)), dma((2, NS, NM)),
     ]
-    return pl.pallas_call(
+    hbm = pl.BlockSpec(memory_space=pltpu.HBM)
+    next_latent, decoded = pl.pallas_call(
         step_kernel,
         out_shape=(
-            jax.ShapeDtypeStruct((1, TOK, 64), F32),
+            jax.ShapeDtypeStruct((1, 64, TOK), F32),
             jax.ShapeDtypeStruct((1, 2, 4, 64, 96), BF16),
         ),
-        in_specs=[pl.BlockSpec(memory_space=pltpu.SMEM)] + [vmem] * 14,
+        in_specs=[hbm] * 15,
         out_specs=(vmem, vmem),
         scratch_shapes=scratch,
         compiler_params=pltpu.CompilerParams(
-            collective_id=0, has_side_effects=True, vmem_limit_bytes=32 * 1024 * 1024
+            collective_id=0, has_side_effects=True, vmem_limit_bytes=60 * 1024 * 1024
         ),
     )(
-        frame_offset, noisy_latent, step_index, query_input, key_input, value_input,
-        context_keys, context_values, query_gain.reshape(1, -1), key_gain.reshape(1, -1),
-        gate_table, head_weight, conv_weight, conv_bias.reshape(1, -1),
+        frame_offset, noisy_latent.transpose(0, 2, 1), step_index, query_input, key_input, value_input,
+        context_keys, context_values, query_gain.reshape(NH, HD), key_gain.reshape(NH, HD),
+        gate_table, head_weight.T, conv_weight, conv_bias.reshape(1, -1),
         jnp.asarray(wave_rows()),
     )
+    return next_latent.transpose(0, 2, 1), decoded
 
 
 def fused_fits(mesh):

time: 36.8 us -> 30.5 us (0.83)
  local copies, waits for them, and re-layouts: 8.52 us -> 2.94 us
  Pallas kernels: 27.1 us -> 26.7 us
    unnamed x27 -> x2, local copies, waits for them, and re-layouts: 7.12 us -> 2.94 us
    pallas_call x1 -> x0, local copies, waits for them, and re-layouts: 0.7 us -> none  [fused_body(): pl.pallas_call(step_kernel, out_shape=(jax.ShapeDtypeStruct((1, TOK, 64),...]
    reshape x2 -> x0, local copies, waits for them, and re-layouts: 0.7 us -> none  [the longest x1 0.7 us: fused_body(): query_gain.reshape(1, -1)]
    pallas_call x1, Pallas kernels: 27.1 us -> 26.7 us  [fused_body(): pl.pallas_call(step_kernel, out_shape=(jax.ShapeDtypeStruct((1, 64, TOK),...]
where the time goes in v2:
time: 30.5 us; the launch traced here: 30.3 us
  Pallas kernels  26.7 us (88%)
  local copies, waits for them, and re-layouts  2.94 us (10%)
  between operations  0.64 us (2%)
    pallas_call x1, Pallas kernels, fused_body(): pl.pallas_call(step_kernel, out_shape=(jax.ShapeDtypeStruct((1, 64, TOK),...  26.7 us
    unnamed x2, local copies, waits for them, and re-layouts  2.94 us

profile of v2, /device:TPU:0, one launch (start us, length us, event | category | flops | bytes accessed | tf_op | source)
XLA Modules:
  0.0 30.3 jit_solution(1658477160091664471)
XLA Ops:
  0.6 26.7 %shard_map.158 = (f32[1,64,128]{2,1,0:T(8,128)}, bf16[1,2,4,64,96]{4,3,2,1,0:T(8,128)(2,1)}) custom-call(s32[4]{0:T(128)} %fo_hbm.1, f32[1,64,128]{2,1,0:T(8,128)} %bitcast.7, s32[1,128]{1,0:T(1,128)} %step_hbm.1, bf16[1,128,640]{2,1,0:T(8,128)(2,1)} %q_hbm.1, bf16[1,128,640]{2,1,0:T(8,128)(2,1)} %k_hbm.1, bf16[1,128,640]{2,1,0:T(8,128)(2,1)} %v_hbm.1, ...), custom_call_target="tpu_custom_call" | custom-call | tf_op jit(solution)/shard_map/pallas_call | solution.py:661
  27.3 1.4 %copy.19 = f32[1,128,64]{1,2,0:T(8,128)} copy(f32[1,128,64]{1,2,0:T(8,128)} %bitcast.8) | data formatting | bytes 65536
  28.7 1.6 %copy.20 = bf16[1,2,4,64,96]{4,3,2,1,0:T(8,128)(2,1)} copy(bf16[1,2,4,64,96]{4,3,2,1,0:T(8,128)(2,1)} %get-tuple-element.9) | data formatting | bytes 196608

commit v3 on v2

--- a/solution.py
+++ b/solution.py
@@ -668,14 +668,14 @@
         out_specs=(vmem, vmem),
         scratch_shapes=scratch,
         compiler_params=pltpu.CompilerParams(
-            collective_id=0, has_side_effects=True, vmem_limit_bytes=60 * 1024 * 1024
+            collective_id=0, has_side_effects=True, vmem_limit_bytes=32 * 1024 * 1024
         ),
-    )(
+    )(*[pltpu.with_memory_space_constraint(x, pltpu.HBM) for x in (
         frame_offset, noisy_latent.transpose(0, 2, 1), step_index, query_input, key_input, value_input,
         context_keys, context_values, query_gain.reshape(NH, HD), key_gain.reshape(NH, HD),
         gate_table, head_weight.T, conv_weight, conv_bias.reshape(1, -1),
         jnp.asarray(wave_rows()),
-    )
+    )])
     return next_latent.transpose(0, 2, 1), decoded
 
 

time: 30.5 us -> 28.1 us (0.921)
  local copies, waits for them, and re-layouts: 2.94 us -> 1.27 us
  Pallas kernels: 26.7 us -> 26 us
    unnamed x2, local copies, waits for them, and re-layouts: 2.94 us -> 1.27 us
    pallas_call x1, Pallas kernels: 26.7 us -> 26 us  [fused_body(): pl.pallas_call(step_kernel, out_shape=(jax.ShapeDtypeStruct((1, 64, TOK),...]
where the time goes in v3:
time: 28.1 us; the launch traced here: 27.9 us
  Pallas kernels  26 us (93%)
  local copies, waits for them, and re-layouts  1.27 us (5%)
  between operations  0.64 us (2%)
    pallas_call x1, Pallas kernels, fused_body(): pl.pallas_call(step_kernel, out_shape=(jax.ShapeDtypeStruct((1, 64, TOK),...  26 us
    unnamed x2, local copies, waits for them, and re-layouts  1.27 us

profile of v3, /device:TPU:0, one launch (start us, length us, event | category | flops | bytes accessed | tf_op | source)
XLA Modules:
  0.0 27.9 jit_solution(8210368592729589624)
XLA Ops:
  0.6 26.0 %shard_map.158 = (f32[1,64,128]{2,1,0:T(8,128)S(1)}, bf16[1,2,4,64,96]{4,3,2,1,0:T(8,128)(2,1)S(1)}) custom-call(s32[4]{0:T(128)} %fo_hbm.1, f32[1,64,128]{2,1,0:T(8,128)} %bitcast.8, s32[1,128]{1,0:T(1,128)} %step_hbm.1, bf16[1,128,640]{2,1,0:T(8,128)(2,1)} %q_hbm.1, bf16[1,128,640]{2,1,0:T(8,128)(2,1)} %k_hbm.1, bf16[1,128,640]{2,1,0:T(8,128)(2,1)} %v_hbm.1, ...), custom_call_target="tpu_custom_call" | custom-call | tf_op jit(solution)/shard_map/pallas_call | solution.py:661
  26.6 0.6 %copy.19 = f32[1,128,64]{1,2,0:T(8,128)} copy(f32[1,128,64]{1,2,0:T(8,128)S(1)} %bitcast.6) | data formatting | bytes 65536
  27.3 0.7 %copy.20 = bf16[1,2,4,64,96]{4,3,2,1,0:T(8,128)(2,1)} copy(bf16[1,2,4,64,96]{4,3,2,1,0:T(8,128)(2,1)S(1)} %get-tuple-element.9) | data formatting | bytes 196608
